TPU v7x, 32 devices: a whole 2x2x4 slice. The times are simulated.
32 devices in a mesh: row: 4 (over y, x), col: 8 (over z, core).
Axes of the slice: x: 2, y: 2, z: 4, core: 2. Of those that a mesh axis runs over, the one named last changes fastest.
Arguments:
- lower_panel: float32 [8, 10, 5, 2, 256, 256], P('col', None, None, None, 'row'), may hold values from -0.0625 to 0.0625
- diag_inverse: float32 [8, 10, 2, 256, 256], P('col', None, None, 'row'), may hold values from -3 to 3, as said below
- structure: int32 [8, 10, 5], P('col'), may hold values 0 or 1
Outputs:
- sel_panel: float32 [8, 10, 5, 2, 256, 256], P('col', None, None, None, 'row')
- sel_diag: float32 [8, 10, 2, 256, 256], P('col', None, None, 'row')
Inputs may be any that keep to these rules, and one draw needn't show every extreme that they name: Every block diag_inverse[c, s, k] equals its own transpose.
All inputs are finite; a program needn't handle non-finite values. No bound on the sum of `structure` on one device may be relied on, other than what follows from the above.
Results may differ from a plain program's by a relative error of at most 0.0001.
Values sent between devices are 32-bit elements; how exact they have to be, the bound alone decides.
No kernel may reach another device: no remote copies, remote signals or barrier semaphores. Data moves between devices by JAX's collectives and lax.ppermute only.
A program may use at most 128 MiB of HBM per device.

v0:
```python
import jax
import jax.numpy as jnp
from jax import lax
from jax.sharding import PartitionSpec as P

LEVELS = 6


def passed_along(value, axis, steps):
    count = lax.axis_size(axis)
    first, last = (max(0, -steps), min(count, count - steps))
    return lax.ppermute(value, axis, [(source, source + steps) for source in range(first, last)])


def chain_apply(parent_chain, panels_full):
    highest = lax.Precision.HIGHEST
    real_part = jnp.einsum(
        "cabpk,cbkj->capj", parent_chain[:, :, :, 0], panels_full[:, :, 0], precision=highest
    ) - jnp.einsum(
        "cabpk,cbkj->capj", parent_chain[:, :, :, 1], panels_full[:, :, 1], precision=highest
    )
    imag_part = jnp.einsum(
        "cabpk,cbkj->capj", parent_chain[:, :, :, 0], panels_full[:, :, 1], precision=highest
    ) + jnp.einsum(
        "cabpk,cbkj->capj", parent_chain[:, :, :, 1], panels_full[:, :, 0], precision=highest
    )
    return jnp.stack([real_part, imag_part], axis=2)


def panel_products(panels, lifted):
    highest = lax.Precision.HIGHEST
    real_part = jnp.einsum(
        "capi,capj->cij", panels[:, :, 0], lifted[:, :, 0], precision=highest
    ) - jnp.einsum("capi,capj->cij", panels[:, :, 1], lifted[:, :, 1], precision=highest)
    imag_part = jnp.einsum(
        "capi,capj->cij", panels[:, :, 0], lifted[:, :, 1], precision=highest
    ) + jnp.einsum("capi,capj->cij", panels[:, :, 1], lifted[:, :, 0], precision=highest)
    return jnp.stack([real_part, imag_part], axis=1)


def lower_pack(chain_new, size_now):
    return jnp.stack(
        [
            chain_new[:, row_pos, col_pos]
            for row_pos in range(size_now)
            for col_pos in range(row_pos + 1)
        ],
        axis=1,
    )


def unpack_lower(packed, size_now):
    order = {}
    for row_pos in range(size_now):
        for col_pos in range(row_pos + 1):
            order[row_pos, col_pos] = len(order)
    strict_list = [(row_pos, col_pos) for row_pos in range(size_now) for col_pos in range(row_pos)]
    flipped = None
    if strict_list:
        pieces = jnp.stack([packed[:, order[key_pair]] for key_pair in strict_list], axis=1)
        swapped = lax.all_to_all(pieces, "row", split_axis=4, concat_axis=3, tiled=True)
        flipped = jnp.swapaxes(swapped, -1, -2)
    block_rows = []
    for row_pos in range(size_now):
        entries = []
        for col_pos in range(size_now):
            if col_pos <= row_pos:
                entries.append(packed[:, order[row_pos, col_pos]])
            else:
                entries.append(flipped[:, strict_list.index((col_pos, row_pos))])
        block_rows.append(jnp.stack(entries, axis=1))
    return jnp.stack(block_rows, axis=1)


def body(lower_panel, diag_inverse, structure):
    columns = lax.axis_size("col")
    position = lax.axis_index("col")
    anc_count = lower_panel.shape[2]
    offset = 0
    parent_chain = None
    panel_parts = []
    diag_parts = []
    for tree_depth in range(LEVELS):
        per_col = max(1, 2**tree_depth // columns)
        if 2**tree_depth <= columns:
            active = (position % (columns // 2**tree_depth) == 0).astype(jnp.float32)
        else:
            active = jnp.ones((), jnp.float32)
        inverse_block = diag_inverse[0, offset : offset + per_col]
        if tree_depth == 0:
            diagonal = inverse_block
            chain_new = inverse_block[:, None, None]
            lifted_pad = jnp.zeros((per_col, anc_count) + inverse_block.shape[1:], jnp.float32)
        else:
            present = structure[0, offset : offset + per_col, :tree_depth].astype(jnp.float32)
            panels = (
                lower_panel[0, offset : offset + per_col, :tree_depth]
                * present[:, :, None, None, None]
            )
            panels_full = lax.all_gather(panels, "row", axis=3, tiled=True)
            lifted = -chain_apply(parent_chain, panels_full)
            diagonal = inverse_block - lax.psum_scatter(
                panel_products(panels, lifted), "row", scatter_dimension=2, tiled=True
            )
            swapped = lax.all_to_all(lifted, "row", split_axis=4, concat_axis=3, tiled=True)
            flipped = jnp.swapaxes(swapped, -1, -2)
            top_row = jnp.concatenate([diagonal[:, None], flipped], axis=1)
            lower_rows = jnp.concatenate([lifted[:, :, None], parent_chain], axis=2)
            chain_new = jnp.concatenate([top_row[:, None], lower_rows], axis=1)
            filler = jnp.zeros(
                (per_col, anc_count - tree_depth) + inverse_block.shape[1:], jnp.float32
            )
            lifted_pad = jnp.concatenate([lifted, filler], axis=1)
        panel_parts.append(lifted_pad * active)
        diag_parts.append(diagonal * active)
        if tree_depth + 1 < LEVELS:
            if 2 ** (tree_depth + 1) <= columns:
                stride = columns // 2 ** (tree_depth + 1)
                parent_here = (position % (2 * stride) == 0).astype(jnp.float32)
                outgoing = chain_new * active
                size_now = tree_depth + 1
                packed = lower_pack(outgoing, size_now)
                arrived = passed_along(packed, "col", stride)
                received = unpack_lower(arrived, size_now)
                parent_chain = received + outgoing * parent_here
            else:
                parent_chain = jnp.repeat(chain_new, 2, axis=0)
        offset = offset + per_col
    sel_panel = jnp.concatenate(panel_parts, axis=0)[None]
    sel_diag = jnp.concatenate(diag_parts, axis=0)[None]
    return (sel_panel, sel_diag)


def solution(mesh):
    in_specs = (
        P("col", None, None, None, "row", None),
        P("col", None, None, "row", None),
        P("col", None, None),
    )
    out_specs = (P("col", None, None, None, "row", None), P("col", None, None, "row", None))
    return jax.shard_map(body, mesh=mesh, in_specs=in_specs, out_specs=out_specs, check_vma=False)
```

profile of v0, /device:TPU:0, one launch (start us, length us, event | category | flops | bytes accessed | tf_op | source)
XLA Modules:
  0.0 496.6 jit_solution(13006598792176292609)
XLA Ops:
  8.8 5.9 %collective-permute-start = (f32[1,1,2,64,256]{4,3,2,1,0:T(8,128)S(1)}, f32[1,1,2,64,256]{4,3,2,1,0:T(8,128)S(1)}, u32[]{:S(2)}, u32[]{:S(2)}) collective-permute-start(f32[1,1,2,64,256]{4,3,2,1,0:T(8,128)S(1)} %get-tuple-element.13), channel_id=1, source_target_pairs={{0,4},{1,5},{2,6},{3,7},{8,12},{9,13},{10,14},{11,15},{16,20},{17,... | collective-permute-start | bytes 393224 | tf_op jit(solution)/shard_map/ppermute | solution.py:12
  18.5 10.1 %all-gather = f32[1,1,1,2,256,256]{5,4,3,2,1,0:T(8,128)S(1)} all-gather(f32[1,1,1,2,64,256]{5,4,3,2,1,0:T(8,128)S(1)} %slice_multiply_fusion), channel_id=2, replica_groups=mesh['row'=4,'col'=8] {'row'}, dimensions={4}, use_global_device_ids=true | all-gather | bytes 655360 | tf_op jit(solution)/shard_map/all_gather | solution.py:100
  35.2 3.3 all-to-all-start
  38.7 5.5 %all-to-all-done = f32[4,1,8192]{2,1,0:T(1,128)S(1)} async-done(((f32[4,1,8192]{2,1,0:T(1,128)}), f32[4,1,8192]{2,1,0:T(1,128)S(1)}, u32[]{:S(2)}, u32[]{:S(2)}) %all-to-all-start) | async-done | bytes 131104 | tf_op jit(solution)/shard_map/all_to_all | solution.py:105
  46.2 9.7 %reduce-scatter.6.cloned.1.call-done = f32[1,2,64,256]{3,2,1,0:T(8,128)} async-done(((f32[1,2,256,256]{3,2,1,0:T(8,128)}), f32[1,2,64,256]{3,2,1,0:T(8,128)}) %reduce-scatter.6.cloned.1.call-update) | async-done | bytes 131088 | tf_op jit(solution)/shard_map/reduce_scatter | solution.py:102
  57.1 3.4 collective-permute-start.1
  60.5 8.2 %collective-permute-done.1 = f32[1,3,2,64,256]{4,3,2,1,0:T(8,128)S(1)} collective-permute-done((f32[1,3,2,64,256]{4,3,2,1,0:T(8,128)S(1)}, f32[1,3,2,64,256]{4,3,2,1,0:T(8,128)S(1)}, u32[]{:S(2)}, u32[]{:S(2)}) %collective-permute-start.1) | collective-permute-done | bytes 393248 | tf_op jit(solution)/shard_map/ppermute | solution.py:12
  69.1 7.5 %all_to_all.108 = f32[4,1,8192]{2,1,0:T(1,128)S(1)} all-to-all(f32[4,1,8192]{2,1,0:T(1,128)S(1)} %reshape.837), channel_id=1, replica_groups=mesh['row'=4,'col'=8] {'row'}, dimensions={0} | all-to-all | bytes 262144 | tf_op jit(solution)/shard_map/all_to_all | solution.py:61
  78.4 6.2 %all-gather.6.cloned.1.call-done = f32[1,2,2,256,256]{4,3,1,2,0:T(8,128)} async-done(((f32[1,2,2,64,256]{4,3,1,2,0:T(8,128)}), f32[1,2,2,256,256]{4,3,1,2,0:T(8,128)}) %all-gather.6.cloned.1.call-update) | async-done | bytes 1048592 | tf_op jit(solution)/shard_map/all_gather | solution.py:100
  92.8 3.4 all-to-all-start.2
  98.3 4.9 all-to-all-done.2
  105.6 11.1 %reduce-scatter.8.cloned.1.call-done = f32[1,2,64,256]{3,2,1,0:T(8,128)} async-done(((f32[1,2,256,256]{3,2,1,0:T(8,128)}), f32[1,2,64,256]{3,2,1,0:T(8,128)}) %reduce-scatter.8.cloned.1.call-update) | async-done | bytes 131088 | tf_op jit(solution)/shard_map/reduce_scatter | solution.py:102
  124.7 3.5 all-to-all-start.3
  129.2 5.9 %all-to-all-done.3 = f32[4,1,24576]{2,1,0:T(1,128)S(1)} async-done(((f32[4,1,24576]{2,1,0:T(1,128)}), f32[4,1,24576]{2,1,0:T(1,128)S(1)}, u32[]{:S(2)}, u32[]{:S(2)}) %all-to-all-start.3) | async-done | bytes 393248 | tf_op jit(solution)/shard_map/all_to_all | solution.py:61
  140.9 9.8 %all-gather.8.cloned.1.call-done = f32[1,3,2,256,256]{4,3,1,2,0:T(8,128)} async-done(((f32[1,3,2,64,256]{4,3,1,2,0:T(8,128)}), f32[1,3,2,256,256]{4,3,1,2,0:T(8,128)}) %all-gather.8.cloned.1.call-update) | async-done | bytes 1572880 | tf_op jit(solution)/shard_map/all_gather | solution.py:100
  163.2 3.5 all-to-all-start.4
  167.9 8.5 %all-to-all-done.4 = f32[4,1,24576]{2,1,0:T(1,128)S(1)} async-done(((f32[4,1,24576]{2,1,0:T(1,128)}), f32[4,1,24576]{2,1,0:T(1,128)S(1)}, u32[]{:S(2)}, u32[]{:S(2)}) %all-to-all-start.4) | async-done | bytes 393248 | tf_op jit(solution)/shard_map/all_to_all | solution.py:105
  182.5 4.1 reduce-scatter.10.cloned.1.call-done
  190.4 50.7 %all-gather.10.cloned.1.call-done = f32[2,4,2,256,256]{4,3,1,0,2:T(8,128)} async-done(((f32[2,4,2,64,256]{4,3,1,0,2:T(8,128)}), f32[2,4,2,256,256]{4,3,1,0,2:T(8,128)}) %all-gather.10.cloned.1.call-update) | async-done | bytes 4194320 | tf_op jit(solution)/shard_map/all_gather | solution.py:100
  241.1 3.7 fusion.21
  257.8 3.6 fusion.4
  270.1 4.4 all-to-all-start.5
  282.4 8.8 %all-to-all-done.5 = f32[4,1,65536]{2,1,0:T(1,128)} async-done(((f32[4,1,65536]{2,1,0:T(1,128)}), f32[4,1,65536]{2,1,0:T(1,128)}, u32[]{:S(2)}, u32[]{:S(2)}) %all-to-all-start.5) | async-done | bytes 1048608 | tf_op jit(solution)/shard_map/all_to_all | solution.py:105
  291.2 4.6 reduce.9
  309.2 89.9 %all-gather.12.cloned.1.call-done = f32[4,5,2,256,256]{4,3,1,0,2:T(8,128)} async-done(((f32[4,5,2,64,256]{4,3,1,0,2:T(8,128)}), f32[4,5,2,256,256]{4,3,1,0,2:T(8,128)}) %all-gather.12.cloned.1.call-update) | async-done | bytes 10485776 | tf_op jit(solution)/shard_map/all_gather | solution.py:100
  399.1 9.7 %broadcast_in_dim.24 = f32[2,2,5,5,2,64,256]{6,5,3,2,1,0,4:T(8,128)} broadcast(f32[2,5,5,2,64,256]{5,4,2,1,0,3:T(8,128)} %maximum_maximum_fusion), dimensions={0,2,3,4,5,6} | broadcast | bytes 19660800 | tf_op jit(solution)/shard_map/broadcast_in_dim | solution.py:127
  408.8 8.8 %fusion.10 = f32[4,5,64,256]{3,2,1,0:T(8,128)S(1)} fusion(f32[4,5,2,256,256]{4,3,1,0,2:T(8,128)S(1)} %copy-done.1, f32[4,5,5,2,64,256]{5,4,2,1,0,3:T(8,128)} %bitcast.595), kind=kOutput, calls=%fused_computation.22 | convolution fusion | flops 5033164800 | bytes 13107200 | tf_op jit(solution)/shard_map/cabpk,cbkj->capj/dot_general | solution.py:24
  417.6 6.1 %fusion.9 = f32[4,5,64,256]{3,2,1,0:T(8,128)S(1)} fusion(f32[4,5,2,256,256]{4,3,1,0,2:T(8,128)S(1)} %copy-done.1, f32[4,5,5,2,64,256]{5,4,2,1,0,3:T(8,128)S(1)} %bitcast.596), kind=kOutput, calls=%fused_computation.21 | convolution fusion | flops 5033164800 | bytes 13107200 | tf_op jit(solution)/shard_map/cabpk,cbkj->capj/dot_general | solution.py:19
  423.7 6.4 %fusion.14 = f32[4,5,1,64,256]{4,3,1,0,2:T(8,128)S(1)} fusion(f32[4,5,64,256]{3,2,1,0:T(8,128)S(1)} %fusion.10, f32[4,5,2,256,256]{4,3,1,0,2:T(8,128)S(1)} %copy-done.1, f32[4,5,5,2,64,256]{5,4,2,1,0,3:T(8,128)S(1)} %bitcast.597), kind=kOutput, calls=%fused_computation.26 | convolution fusion | flops 5033492480 | bytes 14417920 | tf_op jit(solution)/shard_map/cabpk,cbkj->capj/dot_general | solution.py:22
  430.1 6.2 %fusion.16 = f32[4,5,1,64,256]{4,3,1,0,2:T(8,128)S(1)} fusion(f32[4,5,64,256]{3,2,1,0:T(8,128)S(1)} %fusion.9, f32[4,5,2,256,256]{4,3,1,0,2:T(8,128)S(1)} %copy-done.1, f32[4,5,5,2,64,256]{5,4,2,1,0,3:T(8,128)S(1)} %bitcast.598), kind=kOutput, calls=%fused_computation.28 | convolution fusion | flops 5033492480 | bytes 14417920 | tf_op jit(solution)/shard_map/cabpk,cbkj->capj/dot_general | solution.py:17
  452.1 6.6 %copy.164 = f32[1,10,5,2,64,256]{5,4,3,2,1,0:T(8,128)} copy(f32[1,10,5,2,64,256]{5,4,2,1,3,0:T(8,128)} %bitcast.191) | data formatting | bytes 13107200
  458.7 28.7 %reduce-scatter.14.cloned.1.call-done = f32[4,2,64,256]{3,2,0,1:T(8,128)} async-done(((f32[4,2,256,256]{3,2,0,1:T(8,128)}), f32[4,2,64,256]{3,2,0,1:T(8,128)}) %reduce-scatter.14.cloned.1.call-update) | async-done | bytes 524304 | tf_op jit(solution)/shard_map/reduce_scatter | solution.py:102
  (215 shorter events, 128.2 us)
Async XLA Ops:
  7.2 48.8 %reduce-scatter.6.cloned.1.call-start = ((), (), s32[]{:S(2)}) async-start(), calls=%async_computation.11 | async-start | bytes 655360 | tf_op jit(solution)/shard_map/reduce_scatter | solution.py:102
  8.8 19.7 %collective-permute-start = (f32[1,1,2,64,256]{4,3,2,1,0:T(8,128)S(1)}, f32[1,1,2,64,256]{4,3,2,1,0:T(8,128)S(1)}, u32[]{:S(2)}, u32[]{:S(2)}) collective-permute-start(f32[1,1,2,64,256]{4,3,2,1,0:T(8,128)S(1)} %get-tuple-element.13), channel_id=1, source_target_pairs={{0,4},{1,5},{2,6},{3,7},{8,12},{9,13},{10,14},{11,15},{16,20},{17,... | collective-permute-start | bytes 393224 | tf_op jit(solution)/shard_map/ppermute | solution.py:12
  29.3 2.9 copy-start.23
  32.2 52.4 %all-gather.6.cloned.1.call-start = ((), (), s32[]{:S(2)}) async-start(), calls=%async_computation.12 | async-start | bytes 1310720 | tf_op jit(solution)/shard_map/all_gather | solution.py:100
  35.2 8.9 %all-to-all-start = ((f32[4,1,8192]{2,1,0:T(1,128)}), f32[4,1,8192]{2,1,0:T(1,128)S(1)}, u32[]{:S(2)}, u32[]{:S(2)}) async-start(f32[4,1,8192]{2,1,0:T(1,128)} %reshape.835), calls=%async_computation.1 | async-start | bytes 262144 | tf_op jit(solution)/shard_map/all_to_all | solution.py:105
  38.6 78.2 %reduce-scatter.8.cloned.1.call-start = ((), (), s32[]{:S(2)}) async-start(), calls=%async_computation.13 | async-start | bytes 655360 | tf_op jit(solution)/shard_map/reduce_scatter | solution.py:102
  57.1 11.6 %collective-permute-start.1 = (f32[1,3,2,64,256]{4,3,2,1,0:T(8,128)S(1)}, f32[1,3,2,64,256]{4,3,2,1,0:T(8,128)S(1)}, u32[]{:S(2)}, u32[]{:S(2)}) collective-permute-start(f32[1,3,2,64,256]{4,3,2,1,0:T(8,128)S(1)} %pad_maximum_fusion.5), channel_id=1, source_target_pairs={{0,2},{1,3},{2,4},{3,5},{4,6},{5,7},{8,10},{9,11},{10,12},{11,13},... | collective-permute-start | bytes 1179656 | tf_op jit(solution)/shard_map/ppermute | solution.py:12
  78.4 10.1 %copy-start.16 = (f32[1,2,2,64,256]{4,3,1,2,0:T(8,128)S(1)}, f32[1,2,2,64,256]{4,3,1,2,0:T(8,128)}, u32[]{:S(2)}) copy-start(f32[1,2,2,64,256]{4,3,1,2,0:T(8,128)} %fusion.55) | copy-start | bytes 786436
  84.6 3.0 copy-start.15
  92.8 10.4 %all-to-all-start.2 = ((f32[4,1,16384]{2,1,0:T(1,128)}), f32[4,1,16384]{2,1,0:T(1,128)S(1)}, u32[]{:S(2)}, u32[]{:S(2)}) async-start(f32[4,1,16384]{2,1,0:T(1,128)} %reshape.839), calls=%async_computation.4 | async-start | bytes 524288 | tf_op jit(solution)/shard_map/all_to_all | solution.py:105
  96.2 54.5 %all-gather.8.cloned.1.call-start = ((), (), s32[]{:S(2)}) async-start(), calls=%async_computation.14 | async-start | bytes 1966080 | tf_op jit(solution)/shard_map/all_gather | solution.py:100
  118.0 3.5 collective-permute-start.2
  124.7 10.5 %all-to-all-start.3 = ((f32[4,1,24576]{2,1,0:T(1,128)}), f32[4,1,24576]{2,1,0:T(1,128)S(1)}, u32[]{:S(2)}, u32[]{:S(2)}) async-start(f32[4,1,24576]{2,1,0:T(1,128)} %reshape.841), calls=%async_computation.5 | async-start | bytes 786432 | tf_op jit(solution)/shard_map/all_to_all | solution.py:61
  128.1 58.4 %reduce-scatter.10.cloned.1.call-start = ((), (), s32[]{:S(2)}) async-start(), calls=%async_computation.15 | async-start | bytes 655360 | tf_op jit(solution)/shard_map/reduce_scatter | solution.py:102
  137.5 3.2 copy-start.22
  158.3 82.8 %all-gather.10.cloned.1.call-start = ((), (), s32[]{:S(2)}) async-start(), calls=%async_computation.16 | async-start | bytes 5242880 | tf_op jit(solution)/shard_map/all_gather | solution.py:100
  163.2 13.2 %all-to-all-start.4 = ((f32[4,1,24576]{2,1,0:T(1,128)}), f32[4,1,24576]{2,1,0:T(1,128)S(1)}, u32[]{:S(2)}, u32[]{:S(2)}) async-start(f32[4,1,24576]{2,1,0:T(1,128)} %reshape.843), calls=%async_computation.7 | async-start | bytes 786432 | tf_op jit(solution)/shard_map/all_to_all | solution.py:105
  166.7 136.2 %reduce-scatter.12.cloned.1.call-start = ((), (), s32[]{:S(2)}) async-start(), calls=%async_computation.17 | async-start | bytes 1310720 | tf_op jit(solution)/shard_map/reduce_scatter | solution.py:102
  178.7 9.9 %copy-start.19 = (f32[1,3,1,2,64,256]{5,4,3,2,1,0:T(8,128)S(1)}, f32[1,3,1,2,64,256]{5,4,3,2,1,0:T(8,128)}, u32[]{:S(2)}) copy-start(f32[1,3,1,2,64,256]{5,4,3,2,1,0:T(8,128)} %maximum_negate_fusion.4) | copy-start | bytes 1179652
  241.1 3.7 copy-start.5
  250.7 3.7 copy-start.12
  257.6 141.5 %all-gather.12.cloned.1.call-start = ((), (), s32[]{:S(2)}) async-start(), calls=%async_computation.18 | async-start | bytes 13107200 | tf_op jit(solution)/shard_map/all_gather | solution.py:100
  270.1 7.0 %copy-start.4 = (f32[4,4,2,64,256]{4,3,2,1,0:T(8,128)S(1)}, f32[4,4,2,64,256]{4,3,2,1,0:T(8,128)}, u32[]{:S(2)}) copy-start(f32[4,4,2,64,256]{4,3,2,1,0:T(8,128)} %copy-done.3) | copy-start | bytes 6291460
  270.1 21.2 %all-to-all-start.5 = ((f32[4,1,65536]{2,1,0:T(1,128)}), f32[4,1,65536]{2,1,0:T(1,128)}, u32[]{:S(2)}, u32[]{:S(2)}) async-start(f32[4,1,65536]{2,1,0:T(1,128)} %reshape.845), calls=%async_computation.9 | async-start | bytes 2097152 | tf_op jit(solution)/shard_map/all_to_all | solution.py:105
  274.4 213.0 %reduce-scatter.14.cloned.1.call-start = ((), (), s32[]{:S(2)}) async-start(), calls=%async_computation.19 | async-start | bytes 2621440 | tf_op jit(solution)/shard_map/reduce_scatter | solution.py:102
  277.0 3.1 copy-start.11
  277.0 3.1 copy-start.13
  300.0 4.8 copy-start.7
  399.1 9.7 %copy-start.1 = (f32[4,5,2,256,256]{4,3,1,0,2:T(8,128)S(1)}, f32[4,5,2,256,256]{4,3,1,0,2:T(8,128)}, u32[]{:S(2)}) copy-start(f32[4,5,2,256,256]{4,3,1,0,2:T(8,128)} %all-gather.12.cloned.1.call-done) | copy-start | bytes 31457284
  408.8 8.8 %copy-start = (f32[2,2,5,5,2,64,256]{6,5,3,2,1,0,4:T(8,128)S(1)}, f32[2,2,5,5,2,64,256]{6,5,3,2,1,0,4:T(8,128)}, u32[]{:S(2)}) copy-start(f32[2,2,5,5,2,64,256]{6,5,3,2,1,0,4:T(8,128)} %broadcast_in_dim.24) | copy-start | bytes 39321604
  436.3 2.7 copy-start.2
  452.1 35.3 %copy-start.18 = (f32[10,2,64,256]{3,2,0,1:T(8,128)S(1)}, f32[10,2,64,256]{3,2,0,1:T(8,128)}, u32[]{:S(2)}) copy-start(f32[10,2,64,256]{3,2,0,1:T(8,128)} %get-tuple-element.22) | copy-start | bytes 3932164
  (9 other events, 13.8 us)
Sparse Core Ops, SparseCore 0:
  32.3 23.5 reduce-scatter.5
  57.9 26.6 all-gather.5
  91.1 25.6 reduce-scatter.7
  118.5 32.1 all-gather.7
  158.4 28.0 reduce-scatter.9
  188.4 52.6 all-gather.9
  257.7 32.5 reduce-scatter.11
  292.2 106.8 all-gather.11
  452.2 35.1 reduce-scatter.13
where the time goes:
time: 505 us; the launch traced here: 497 us
  waiting for transfers between devices  254 us (50%)
  matrix products  67.6 us (13%)
  local copies, waits for them, and re-layouts  60.4 us (12%)
  other arithmetic  51.2 us (10%)
  starting transfers between devices  30 us (6%)
  blocking collectives  17.6 us (3%)
  between operations  15.8 us (3%)
    all_gather x4, waiting for transfers between devices, body(): panels_full = lax.all_gather(panels, 'row', axis=3, tiled=True)  157 us
    reduce_scatter x5, waiting for transfers between devices, body(): lax.psum_scatter(panel_products(panels, lifted), 'row', scatter_dimension...  53.7 us
    all_to_all x4, waiting for transfers between devices, body(): lax.all_to_all(lifted, 'row', split_axis=4, concat_axis=3, tiled=True)  27.7 us
    unnamed x72, local copies, waits for them, and re-layouts  27.7 us
    dot_general x10, matrix products, chain_apply(): jnp.einsum('cabpk,cbkj->capj', parent_chain[:, :, :, 1], panels_full[:, :...  26.6 us
    dot_general x10, matrix products, chain_apply(): jnp.einsum('cabpk,cbkj->capj', parent_chain[:, :, :, 0], panels_full[:, :...  19.1 us
    all_to_all x4, starting transfers between devices, body(): lax.all_to_all(lifted, 'row', split_axis=4, concat_axis=3, tiled=True)  14.6 us
    mul x6, other arithmetic, body(): lower_panel[0, offset:offset + per_col, :tree_depth]  11.5 us
  transfers between devices with their start and end apart: 17, of which 15 were waited for; matrix products, arithmetic and copies ran while one was open for 16% of the time, Pallas kernels for 0%

commit v1 on v0

v1 whole, which is shorter than its diff:
```python
import functools

import jax
import jax.numpy as jnp
from jax import lax
from jax.experimental import pallas as pl
from jax.experimental.pallas import tpu as pltpu
from jax.sharding import PartitionSpec as P

LEVELS = 6
HALVES = 2
VMEM_BYTES = 56 * 2**20
F32 = jnp.float32
BF16 = jnp.bfloat16
ANY = pl.BlockSpec(memory_space=pl.ANY)
VMEM = pl.BlockSpec(memory_space=pltpu.VMEM)
SMEM = pl.BlockSpec(memory_space=pltpu.SMEM)


def xor_swap(value, axis, mask):
    count = lax.axis_size(axis)
    return lax.ppermute(value, axis, [(source, source ^ mask) for source in range(count)])


def split(value):
    high = value.astype(BF16)
    return high, (value - high.astype(F32)).astype(BF16)


def three_products(left_high, left_low, right_high, right_low):
    left = jnp.concatenate([left_high, left_high, left_low], axis=1)
    right = jnp.concatenate([right_high, right_low, right_high], axis=0)
    return jnp.dot(left, right, preferred_element_type=F32)


def complex_sum(product, half):
    count = product.shape[0] // 2
    by_real, by_imag = product[:count], product[count:]
    return jnp.concatenate(
        [by_real[:, :half] - by_imag[:, half:], by_real[:, half:] + by_imag[:, :half]], axis=1
    )


def run_kernel(kernel, outs, ins, scratch, flops, aliases=None):
    moved = sum(value.size for value, _ in ins)
    return pl.pallas_call(
        kernel,
        out_shape=[jax.ShapeDtypeStruct(shape, dtype) for shape, dtype, _ in outs],
        in_specs=[spec for _, spec in ins],
        out_specs=[spec for _, _, spec in outs],
        scratch_shapes=scratch,
        input_output_aliases=aliases or {},
        compiler_params=pltpu.CompilerParams(vmem_limit_bytes=VMEM_BYTES),
        cost_estimate=pl.CostEstimate(flops=flops, bytes_accessed=2 * moved, transcendentals=0),
    )(*[value for value, _ in ins])


class Loads:
    def __init__(self, sources, buffers, sems):
        self.buffers = buffers
        self.copies = [
            pltpu.make_async_copy(source, buffer, sems.at[at])
            for at, (source, buffer) in enumerate(zip(sources, buffers))
        ]
        for copy in self.copies:
            copy.start()

    def get(self, at):
        if self.copies[at] is not None:
            self.copies[at].wait()
            self.copies[at] = None
        return self.buffers[at]


def both_parts(mask, array, base=0):
    return [(mask, 0, array, 2 * base, 2), (mask, 1, array, 2 * base + 1, 2)]


def pack_kernel(spans, plan, n_outs, chunk, *refs):
    scalars, present, panel_ref, diag_ref = refs[:4]
    outs = refs[4 : 4 + n_outs]
    panel_bufs = refs[4 + n_outs : -2]
    diag_buf, sems = refs[-2:]
    sources, buffers = [], []
    for (first, nodes, depth), buffer in zip(spans, panel_bufs):
        sources.append(panel_ref.at[0, pl.ds(first, nodes), pl.ds(0, depth)])
        buffers.append(buffer)
    if any(block == 0 for blocks in plan for _, _, block in blocks):
        sources.append(diag_ref.at[0])
        buffers.append(diag_buf)
    loads = Loads(sources, buffers, sems)
    where = {first: at for at, (first, _, _) in enumerate(spans)}
    for out, blocks in zip(outs, plan):
        for at, (first, node_of, block) in enumerate(blocks):
            node = node_of(scalars[0])
            if block == 0:
                value = loads.get(len(spans))[first + node]
            else:
                scale = present[first + node, block - 1].astype(F32)
                value = loads.get(where[first])[node, block - 1] * scale
            out[pl.ds(2 * at, 2)] = value


def pack(plan, spans, scalars, present, lower_panel, diag_inverse):
    chunk, width = lower_panel.shape[-2:]
    outs = [((2 * len(blocks), chunk, width), F32, VMEM) for blocks in plan]
    scratch = [pltpu.VMEM((nodes, depth, 2, chunk, width), F32) for _, nodes, depth in spans]
    scratch += [pltpu.VMEM(diag_inverse.shape[1:], F32), pltpu.SemaphoreType.DMA((len(spans) + 1,))]
    kernel = functools.partial(pack_kernel, spans, plan, len(outs), chunk)
    ins = [(scalars, SMEM), (present, SMEM), (lower_panel, ANY), (diag_inverse, ANY)]
    return run_kernel(kernel, outs, ins, scratch, 0)


def pack_last_kernel(first, nodes, depth, steps, cols, *refs):
    scalars, present, panel_ref = refs[:3]
    outs = refs[3 : 3 + len(steps) * HALVES]
    buffer, sem = refs[-2:]
    copy = pltpu.make_async_copy(panel_ref.at[0, pl.ds(first, nodes), pl.ds(0, depth)], buffer, sem)
    copy.start()
    copy.wait()
    for at, (step, group) in enumerate(steps):
        node = (scalars[0] // group) ^ step
        for block in range(depth):
            value = buffer[node, block] * present[first + node, block].astype(F32)
            for half in range(HALVES):
                outs[half * len(steps) + at][pl.ds(2 * block, 2)] = value[
                    :, :, half * cols : (half + 1) * cols
                ]


def pack_last(first, nodes, depth, steps, cols, scalars, present, lower_panel):
    chunk, width = lower_panel.shape[-2:]
    outs = [((2 * depth, chunk, cols), F32, VMEM)] * (len(steps) * HALVES)
    scratch = [pltpu.VMEM((nodes, depth, 2, chunk, width), F32), pltpu.SemaphoreType.DMA]
    kernel = functools.partial(pack_last_kernel, first, nodes, depth, steps, cols)
    ins = [(scalars, SMEM), (present, SMEM), (lower_panel, ANY)]
    return run_kernel(kernel, outs, ins, scratch, 0)


def prep_kernel(levels, table, chunk, width, n_arrays, *refs):
    scalars = refs[0]
    arrays = refs[1 : 1 + n_arrays]
    outs = list(refs[1 + n_arrays :])
    place = scalars[0]
    odd = scalars[1] == 1
    for depth, swapped, first in levels:
        if depth:
            whole, fwd_high, fwd_low = outs.pop(0), outs.pop(0), outs.pop(0)
        else:
            whole = None
        back_high, back_low = outs.pop(0), outs.pop(0)
        for block in range(depth + 1):
            for mask, part, position, base, stride in table:
                plane = base + stride * (first + block)
                if swapped is None:
                    value = arrays[position][plane]
                else:
                    half = n_arrays // 2
                    from_odd = arrays[position + (0 if swapped else half)]
                    from_even = arrays[position + (half if swapped else 0)]
                    value = jnp.where(odd, from_odd[plane], from_even[plane])
                start = pl.multiple_of((place ^ mask) * chunk, chunk)
                if block == 0:
                    high, low = split(value)
                    lanes = pl.ds(depth * width, width)
                    rows = pl.ds(pl.multiple_of(part * width + start, chunk), chunk)
                    back_high[rows, lanes] = high
                    back_low[rows, lanes] = low
                else:
                    rows = pl.ds(pl.multiple_of((depth - block) * width + start, chunk), chunk)
                    whole[rows, pl.ds(part * width, width)] = value
        for level in range(depth):
            for part in range(2):
                value = whole[pl.ds(level * width, width), pl.ds(part * width, width)]
                high, low = split(value)
                rows = pl.ds((2 * level + part) * width, width)
                fwd_high[rows] = high
                fwd_low[rows] = low
                high, low = split(-value.T)
                rows, lanes = pl.ds(part * width, width), pl.ds(level * width, width)
                back_high[rows, lanes] = high
                back_low[rows, lanes] = low


def prep(levels, pieces, scalars, chunk, width, others=()):
    arrays, table = [], []
    for mask, part, array, base, stride in pieces:
        position = next((at for at, value in enumerate(arrays) if value is array), None)
        if position is None:
            position = len(arrays)
            arrays.append(array)
        table.append((mask, part, position, base, stride))
    arrays = arrays + list(others)
    outs = []
    for depth, _, _ in levels:
        if depth:
            outs.append(((depth * width, 2 * width), F32, VMEM))
            outs += [((2 * depth * width, width), BF16, VMEM)] * 2
        outs += [((2 * width, (depth + 1) * width), BF16, VMEM)] * 2
    kernel = functools.partial(prep_kernel, levels, table, chunk, width, len(arrays))
    ins = [(scalars, SMEM)] + [(value, VMEM) for value in arrays]
    made = list(run_kernel(kernel, outs, ins, [], 0))
    result = {}
    for depth, _, _ in levels:
        if depth:
            result[depth], made = tuple(made[:5]), made[5:]
        else:
            result[depth], made = (None, None, None) + tuple(made[:2]), made[2:]
    return result


def substitute(depth, width, cols, forward, backward, sums, right_high, right_low, emit):
    def rows(first, count=1):
        return pl.ds(first * width, count * width)

    for level in range(depth - 1, 0, -1):
        high, low = split(sums[rows(level)])
        right_high[rows(level)] = high
        right_low[rows(level)] = low
        fwd_high, fwd_low = forward(level)
        for block in range(level - 1, -1, -1):
            product = three_products(
                fwd_high[rows(2 * block, 2)], fwd_low[rows(2 * block, 2)], high, low
            )
            sums[rows(block)] -= complex_sum(product, cols)
    high, low = split(sums[rows(0)])
    right_high[rows(0)] = high
    right_low[rows(0)] = low
    for level in range(depth):
        back_high, back_low = backward(level)
        product = three_products(
            back_high[...],
            back_low[...],
            right_high[rows(0, level + 1)],
            right_low[rows(0, level + 1)],
        )
        solved = complex_sum(product, cols)
        high, low = split(solved)
        right_high[rows(level)] = high
        right_low[rows(level)] = low
        emit(level, solved)


def solve_kernel(depths, chunk, width, steps, order, masked, *refs):
    refs = list(refs)
    scalars = refs.pop(0)
    sources = [refs.pop(0) for _ in order]
    outs = {depth: [(refs.pop(0), refs.pop(0)) for _ in steps] for depth in depths}
    buffers = [refs.pop(0) for _ in order]
    sems, sums_ref, high_ref, low_ref, solved_ref = refs
    loads = Loads(sources, buffers, sems)

    def get(kind, level):
        return loads.get(order.index((kind, level)))

    place = scalars[0]
    for depth in depths:
        span = pl.ds(0, depth * width)
        sums, right_high, right_low = sums_ref.at[span], high_ref.at[span], low_ref.at[span]
        sums[...] = get("whole", depth)[...]

        def send(block, value, sign):
            solved_ref[...] = value
            for (out, correction), step in zip(outs[depth], steps):
                start = pl.multiple_of((place ^ step) * chunk, chunk)
                piece = solved_ref[pl.ds(start, chunk)] * sign
                if depth in masked:
                    piece = jnp.where(scalars[2 + depth] == 1, piece, 0.0)
                for part in range(2):
                    plane = piece[:, part * width : (part + 1) * width]
                    if block == 0:
                        correction[part] = plane
                    else:
                        out[block - 1, part] = plane

        substitute(
            depth, width, width,
            lambda level: (get("fh", level), get("fl", level)),
            lambda level: (get("bh", level), get("bl", level)),
            sums, right_high, right_low,
            lambda level, solved: send(depth - level, solved, -1.0),
        )
        back_high, back_low = get("bh", depth), get("bl", depth)
        product = three_products(
            back_high[:, : depth * width], back_low[:, : depth * width],
            right_high[...], right_low[...],
        )
        send(0, complex_sum(product, width), 1.0)


def operands(made, names):
    index = {"whole": 0, "fh": 1, "fl": 2, "bh": 3, "bl": 4}
    return [made[level][index[kind]] for kind, level in names]


def solve(depths, made, scalars, steps, chunk, width, masked):
    top = depths[0]
    order = [("whole", top)]
    for level in range(top - 1, 0, -1):
        order += [("fh", level), ("fl", level)]
    for level in range(top + 1):
        order += [("bh", level), ("bl", level)]
    order += [("whole", depth) for depth in depths[1:]]
    sources = operands(made, order)
    outs = []
    for depth in depths:
        for _ in steps:
            outs.append(((depth, 2, chunk, width), F32, VMEM))
            outs.append(((2, chunk, width), F32, VMEM))
    scratch = [pltpu.VMEM(value.shape, value.dtype) for value in sources]
    scratch += [
        pltpu.SemaphoreType.DMA((len(order),)),
        pltpu.VMEM((top * width, 2 * width), F32),
        pltpu.VMEM((top * width, 2 * width), BF16),
        pltpu.VMEM((top * width, 2 * width), BF16),
        pltpu.VMEM((width, 2 * width), F32),
    ]
    kernel = functools.partial(solve_kernel, depths, chunk, width, steps, order, masked)
    flops = sum(24 * (depth * depth + depth) * width**3 for depth in depths)
    ins = [(scalars, SMEM)] + [(value, ANY) for value in sources]
    got = list(run_kernel(kernel, outs, ins, scratch, flops))
    result = {}
    for depth in depths:
        result[depth] = [(got.pop(0), got.pop(0)) for _ in steps]
    return result


def last_kernel(depth, chunk, width, cols, steps, table, n_arrays, order, *refs):
    refs = list(refs)
    scalars = refs.pop(0)
    arrays = [refs.pop(0) for _ in range(n_arrays)]
    sources = [refs.pop(0) for _ in order]
    outs = [refs.pop(0) for _ in steps]
    left_high, left_low, right_high, right_low = (refs.pop(0) for _ in range(4))
    buffers = [refs.pop(0) for _ in order]
    sems, sums, solved_ref = refs
    loads = Loads(sources, buffers, sems)

    def get(kind, level):
        return loads.get(order.index((kind, level)))

    place = scalars[0]
    for mask, part, position, base, stride in table:
        start = pl.multiple_of((place ^ mask) * chunk, chunk)
        for block in range(depth):
            row = pl.multiple_of((depth - 1 - block) * width + start, chunk)
            sums[pl.ds(row, chunk), pl.ds(part * cols, cols)] = arrays[position][base + stride * block]
    for level in range(depth):
        for part in range(2):
            value = sums[pl.ds(level * width, width), pl.ds(part * cols, cols)]
            high, low = split(value.T)
            rows, lanes = pl.ds(part * cols, cols), pl.ds(level * width, width)
            left_high[rows, lanes] = high
            left_low[rows, lanes] = low

    def emit(level, value):
        solved_ref[...] = value
        for out, step in zip(outs, steps):
            start = pl.multiple_of((place ^ step) * chunk, chunk)
            piece = -solved_ref[pl.ds(start, chunk)]
            out[depth - 1 - level, 0] = piece[:, :cols]
            out[depth - 1 - level, 1] = piece[:, cols:]

    substitute(
        depth, width, cols,
        lambda level: (get("fh", level), get("fl", level)),
        lambda level: (get("bh", level), get("bl", level)),
        sums, right_high, right_low, emit,
    )


def solve_last(depth, made, pieces, scalars, steps, chunk, width, cols):
    arrays, table = [], []
    for mask, part, array, base, stride in pieces:
        position = next((at for at, value in enumerate(arrays) if value is array), None)
        if position is None:
            position = len(arrays)
            arrays.append(array)
        table.append((mask, part, position, base, stride))
    order = []
    for level in range(depth - 1, 0, -1):
        order += [("fh", level), ("fl", level)]
    for level in range(depth):
        order += [("bh", level), ("bl", level)]
    sources = operands(made, order)
    outs = [((depth, 2, chunk, cols), F32, VMEM)] * len(steps)
    outs += [((2 * cols, depth * width), BF16, VMEM)] * 2
    outs += [((depth * width, 2 * cols), BF16, VMEM)] * 2
    scratch = [pltpu.VMEM(value.shape, value.dtype) for value in sources]
    scratch += [
        pltpu.SemaphoreType.DMA((len(order),)),
        pltpu.VMEM((depth * width, 2 * cols), F32),
        pltpu.VMEM((width, 2 * cols), F32),
    ]
    kernel = functools.partial(
        last_kernel, depth, chunk, width, cols, steps, table, len(arrays), order
    )
    flops = 24 * depth * depth * width * width * cols
    ins = [(scalars, SMEM)] + [(value, VMEM) for value in arrays]
    ins += [(value, ANY) for value in sources]
    got = run_kernel(kernel, outs, ins, scratch, flops)
    return got[: len(steps)], got[len(steps) :]


def correction_kernel(chunk, width, cols, steps, parts, *refs):
    refs = list(refs)
    scalars = refs.pop(0)
    lefts = [tuple(refs.pop(0) for _ in range(4)) for _ in range(parts)]
    outs = [refs.pop(0) for _ in steps]
    (total,) = refs
    place = scalars[0]
    product = three_products(
        jnp.concatenate([left[0][...] for left in lefts], axis=0),
        jnp.concatenate([left[1][...] for left in lefts], axis=0),
        jnp.concatenate([left[2][...] for left in lefts], axis=1),
        jnp.concatenate([left[3][...] for left in lefts], axis=1),
    )
    size = 2 * cols
    for row in range(parts):
        for col in range(parts):
            block = product[row * size : (row + 1) * size, col * size : (col + 1) * size]
            block = -complex_sum(block, cols)
            rows, lanes = pl.ds(row * cols, cols), pl.ds(col * cols, cols)
            total[0, rows, lanes] = block[:, :cols]
            total[1, rows, lanes] = block[:, cols:]
    for out, step in zip(outs, steps):
        start = pl.multiple_of((place ^ step) * chunk, chunk)
        out[0] = total[0, pl.ds(start, chunk)]
        out[1] = total[1, pl.ds(start, chunk)]


def last_correction(lefts, scalars, steps, chunk, width, cols):
    outs = [((2, chunk, width), F32, VMEM)] * len(steps)
    kernel = functools.partial(correction_kernel, chunk, width, cols, steps, len(lefts))
    flops = 24 * lefts[0][2].shape[0] * width * width
    ins = [(scalars, SMEM)] + [(value, VMEM) for left in lefts for value in left]
    return run_kernel(kernel, outs, ins, [pltpu.VMEM((2, width, width), F32)], flops)


def begin_kernel(plan, zeros, *refs):
    scalars = refs[0]
    pieces = refs[1 : 1 + len(plan)]
    out, zero_ref, sem = refs[1 + len(plan) :]
    zero_ref[...] = jnp.zeros_like(zero_ref)
    copies = []
    for slot, depth, count in zeros:
        copies.append((zero_ref.at[pl.ds(0, count)], out.at[0, slot, pl.ds(depth, count)]))
    for piece, (first, group, step, depth) in zip(pieces, plan):
        slot = first + ((scalars[0] // group) ^ step)
        copies.append((piece, out.at[0, slot, pl.ds(0, depth)]))
    copies = [
        pltpu.make_async_copy(source, target, sem.at[at])
        for at, (source, target) in enumerate(copies)
    ]
    for copy in copies:
        copy.start()
    for copy in copies:
        copy.wait()


def place_kernel(plan, cols, half, *refs):
    scalars = refs[0]
    pieces = refs[1 : 1 + len(plan)]
    out, sem = refs[-2:]
    copies = []
    for at, (piece, (first, group, step)) in enumerate(zip(pieces, plan)):
        slot = first + ((scalars[0] // group) ^ step)
        target = out.at[0, slot, :, :, :, pl.ds(half * cols, cols)]
        copies.append(pltpu.make_async_copy(piece, target, sem.at[at]))
    for copy in copies:
        copy.start()
    for copy in copies:
        copy.wait()


def diagonal_kernel(plan, shared, *refs):
    scalars, own = refs[:2]
    pieces = refs[2 : 2 + len(plan)]
    out = refs[-1]
    for slot in range(out.shape[1]):
        value = own[0, slot]
        if slot in shared:
            value = jnp.where(scalars[2 + shared[slot]] == 1, value, 0.0)
        out[0, slot] = value
    for piece, (first, group, step) in zip(pieces, plan):
        slot = first + ((scalars[0] // group) ^ step)
        out[0, slot] = out[0, slot] - piece[...]


def body(lower_panel, diag_inverse, structure):
    columns = lax.axis_size("col")
    rows = lax.axis_size("row")
    position = lax.axis_index("col")
    place = lax.axis_index("row")
    slots, anc_count, _, chunk, width = lower_panel.shape[1:]
    per_col = [max(1, 2**depth // columns) for depth in range(LEVELS)]
    offsets = [sum(per_col[:depth]) for depth in range(LEVELS)]
    last = LEVELS - 1
    cols = width // HALVES
    groups = [rows // nodes for nodes in per_col]
    steps = [[step * groups[depth] for step in range(per_col[depth])] for depth in range(LEVELS)]
    shared = [depth for depth in range(LEVELS) if 2**depth < columns]
    middle = [depth for depth in range(LEVELS - 1) if 2**depth >= columns]
    active = [position % max(1, columns // 2**depth) == 0 for depth in range(LEVELS)]
    scalars = jnp.stack([place, position % 2] + active).astype(jnp.int32)
    present = structure[0]

    upper = shared[:-1]
    starts = [sum(1 + depth for depth in upper[:at]) for at in range(len(upper))]

    def level_blocks(depth, step=0):
        group = groups[depth]
        return [
            (offsets[depth], lambda at, group=group, step=step: (at // group) ^ step, block)
            for block in range(depth + 1)
        ]

    near_plan, far_plan = [], []
    bases = {}
    for depth in middle:
        bases[depth] = len(near_plan)
        near_plan += level_blocks(depth)
        far_plan += level_blocks(depth, 0 if groups[depth] > 2 else 1)
    plan = [sum([level_blocks(depth) for depth in upper], []), level_blocks(shared[-1])]
    if middle:
        plan += [near_plan, far_plan]
    spans = [
        (offsets[depth], per_col[depth], depth) for depth in shared[1:] + middle
    ]
    packed = list(pack(plan, spans, scalars, present, lower_panel, diag_inverse))
    upper_pack, own_pack = packed[:2]

    stride = columns // 2
    while stride >= 4:
        held = [at for at, depth in enumerate(upper) if columns // 2**depth >= 2 * stride]
        count = 2 * (starts[held[-1]] + 1 + upper[held[-1]])
        pairs = [(source, source + stride) for source in range(0, columns, 2 * stride)]
        if stride == columns // 2 and count == 2:
            travelling = diag_inverse[0, 0]
        else:
            travelling = upper_pack[:count]
        arrived = lax.ppermute(travelling, "col", pairs)
        fresh = position % (2 * stride) == stride
        upper_pack = jnp.concatenate(
            [jnp.where(fresh, arrived, upper_pack[:count]), upper_pack[count:]], axis=0
        )
        stride //= 2
    from_one = lax.ppermute(
        upper_pack, "col", [(source, source + 1) for source in range(0, columns, 4)]
    )
    from_three = lax.ppermute(
        upper_pack, "col", [(source, source + 3) for source in range(0, columns, 4)]
    )
    upper_got = jnp.where(position % 4 == 1, from_one, from_three)
    planes = max(own_pack.shape[0], upper_got.shape[0])

    def fill(value):
        return jnp.pad(value, ((0, planes - value.shape[0]), (0, 0), (0, 0)))

    own = jnp.where(position % 2 == 1, fill(upper_got), fill(own_pack))

    if middle:
        near_pack, far_pack = packed[2:]
        near_got = xor_swap(near_pack, "row", 1)
        far_got = xor_swap(far_pack, "row", 2)
    near = xor_swap(own, "row", 1)
    far = xor_swap(own, "row", 2)
    far_split = far.reshape(planes // 2, 2, chunk, width)
    near_split = near.reshape(planes // 2, 2, chunk, width)
    near_sends, far_sends = [far_split[:, 0]], [near_split[:, 1]]
    homes = {}
    near_size = far_size = planes // 2
    for depth in middle:
        first, count = 2 * bases[depth], 2 * (depth + 1)
        homes[depth] = (near_size, far_size)
        if groups[depth] > 2:
            far_level = far_got[first : first + count].reshape(depth + 1, 2, chunk, width)
            near_level = near_got[first : first + count].reshape(depth + 1, 2, chunk, width)
            near_sends.append(far_level[:, 0])
            far_sends.append(near_level[:, 1])
            near_size += depth + 1
            far_size += depth + 1
        else:
            near_sends.append(far_got[first : first + count])
            near_size += count
    near_more = xor_swap(jnp.concatenate(near_sends, axis=0), "row", 1)
    far_more = xor_swap(jnp.concatenate(far_sends, axis=0), "row", 2)

    blocks = planes // 2
    mine = jnp.concatenate([own, near, far, near_more[:blocks], far_more[:blocks]], axis=0)
    theirs = xor_swap(mine, "col", 1)
    shared_pieces = (
        both_parts(0, mine)
        + both_parts(1, mine, blocks)
        + both_parts(2, mine, 2 * blocks)
        + [(3, 0, mine, 6 * blocks, 1), (3, 1, mine, 7 * blocks, 1)]
    )

    made = {}
    for depth in middle:
        base = bases[depth]
        near_home, far_home = homes[depth]
        pieces = both_parts(0, near_pack, base) + both_parts(1, near_got, base)
        pieces += both_parts(2, far_got, base)
        if groups[depth] > 2:
            pieces += [(3, 0, near_more, near_home, 1), (3, 1, far_more, far_home, 1)]
        else:
            pieces += [(3, 0, near_more, near_home, 2), (3, 1, near_more, near_home + 1, 2)]
        made.update(prep([(depth, None, 0)], pieces, scalars, chunk, width))
    levels = [(depth, True, starts[at]) for at, depth in enumerate(upper)]
    levels.append((shared[-1], False, 0))
    made.update(prep(levels, shared_pieces, scalars, chunk, width, others=[theirs]))

    nodes, group = per_col[last], groups[last]
    last_packs = pack_last(
        offsets[last], nodes, last, [(step, group) for step in range(nodes)], cols,
        scalars, present, lower_panel,
    )
    last_pieces = []
    for half in range(HALVES):
        packs = last_packs[half * nodes : (half + 1) * nodes]
        if half == 0:
            packs, _ = lax.optimization_barrier((packs, near))
        else:
            packs, _ = lax.optimization_barrier((packs, near_more))
        pieces = []
        for step, value in zip(steps[last], packs):
            arrived = xor_swap(value, "row", step) if step else value
            if group == 1:
                pieces += both_parts(step, arrived)
                continue
            listed = [(step, arrived)]
            mask = 1
            while mask < group:
                listed += [(mask | at, xor_swap(held, "row", mask)) for at, held in listed]
                mask *= 2
            for at, held in listed:
                pieces += both_parts(at, held)
        last_pieces.append(pieces)

    lefts, backs = [], []
    for half in range(HALVES):
        outward, left = solve_last(
            last, made, last_pieces[half], scalars, steps[last], chunk, width, cols
        )
        lefts.append(left)
        backs.append(
            [xor_swap(piece, "row", step) if step else piece for piece, step in zip(outward, steps[last])]
        )
    corrections = last_correction(lefts, scalars, steps[last], chunk, width, cols)
    corrections = [
        xor_swap(piece, "row", step) if step else piece
        for piece, step in zip(corrections, steps[last])
    ]

    single = [depth for depth in range(last - 1, 0, -1) if per_col[depth] == 1]
    solved = {}
    for depth in range(1, last):
        if per_col[depth] > 1:
            solved.update(solve([depth], made, scalars, steps[depth], chunk, width, ()))
    solved.update(solve(single, made, scalars, [0], chunk, width, tuple(shared)))

    begin_plan, begin_pieces, diag_plan, diag_pieces = [], [], [], []
    for depth in range(1, last):
        for step, (piece, correction) in enumerate(solved[depth]):
            if step:
                both = jnp.concatenate([piece, correction[None]], axis=0)
                both = xor_swap(both, "row", steps[depth][step])
                piece, correction = both[:depth], both[depth]
            begin_plan.append((offsets[depth], groups[depth], step, depth))
            begin_pieces.append(piece)
            diag_plan.append((offsets[depth], groups[depth], step))
            diag_pieces.append(correction)
    zeros = [
        (offsets[depth] + node, depth, anc_count - depth)
        for depth in range(LEVELS)
        for node in range(per_col[depth])
        if depth < anc_count
    ]
    panel_shape = lower_panel.shape
    (sel_panel,) = run_kernel(
        functools.partial(begin_kernel, begin_plan, zeros),
        [(panel_shape, F32, ANY)],
        [(scalars, SMEM)] + [(piece, VMEM) for piece in begin_pieces],
        [
            pltpu.VMEM((anc_count, 2, chunk, width), F32),
            pltpu.SemaphoreType.DMA((len(zeros) + len(begin_plan),)),
        ],
        0,
    )
    last_plan = [(offsets[last], group, step) for step in range(nodes)]
    for half, back in enumerate(backs):
        def write(scalar_ref, *refs, half=half):
            place_kernel(last_plan, cols, half, scalar_ref, *refs[:nodes], *refs[nodes + 1 :])

        (sel_panel,) = run_kernel(
            write,
            [(panel_shape, F32, ANY)],
            [(scalars, SMEM)] + [(piece, ANY) for piece in back] + [(sel_panel, ANY)],
            [pltpu.SemaphoreType.DMA((nodes,))],
            0,
            aliases={1 + nodes: 0},
        )
    diag_plan += last_plan
    diag_pieces += list(corrections)
    (sel_diag,) = run_kernel(
        functools.partial(diagonal_kernel, diag_plan, {offsets[depth]: depth for depth in shared}),
        [(diag_inverse.shape, F32, VMEM)],
        [(scalars, SMEM), (diag_inverse, VMEM)] + [(piece, VMEM) for piece in diag_pieces],
        [],
        0,
    )
    return (sel_panel, sel_diag)


def solution(mesh):
    in_specs = (
        P("col", None, None, None, "row", None),
        P("col", None, None, "row", None),
        P("col", None, None),
    )
    out_specs = (P("col", None, None, None, "row", None), P("col", None, None, "row", None))
    return jax.shard_map(body, mesh=mesh, in_specs=in_specs, out_specs=out_specs, check_vma=False)
```

time: 505 us -> 296 us (0.59); the launches traced: 497 us -> 295 us
  waiting for transfers between devices: 254 us -> 54.4 us
  Pallas kernels: 0 us -> 192 us
  matrix products: 67.6 us -> 0 us
  local copies, waits for them, and re-layouts: 60.4 us -> 10.4 us
  other arithmetic: 51.2 us -> 3.17 us
  blocking collectives: 17.6 us -> 0 us
  between operations: 15.8 us -> 1.17 us
    pallas_call x0 -> x14, Pallas kernels: none -> 192 us  [run_kernel(): pl.pallas_call(kernel, out_shape=[jax.ShapeDtypeStruct(shape, dtype) for...]
    all_gather x4 -> x0, waiting for transfers between devices: 157 us -> none  [body(): panels_full = lax.all_gather(panels, 'row', axis=3, tiled=True)]
    dot_general x40 -> x0, matrix products: 67.6 us -> none  [the longest x10 26.6 us: chain_apply(): jnp.einsum('cabpk,cbkj->capj', parent_chain[:, :, :, 1], panels_full[:, :...]
    reduce_scatter x5 -> x0, waiting for transfers between devices: 53.7 us -> none  [body(): lax.psum_scatter(panel_products(panels, lifted), 'row', scatter_dimension...]
    ppermute x3 -> x26, waiting for transfers between devices: 10 us -> 54.4 us  [the longest x23 51.7 us: xor_swap(): lax.ppermute(value, axis, [(source, source ^ mask) for source in range(co...]
    all_to_all x5 -> x0, waiting for transfers between devices: 33.6 us -> none  [the longest x4 27.7 us: body(): lax.all_to_all(lifted, 'row', split_axis=4, concat_axis=3, tiled=True)]
    ppermute x3 -> x26, starting transfers between devices: 11 us -> 34.6 us  [the longest x23 26 us: xor_swap(): lax.ppermute(value, axis, [(source, source ^ mask) for source in range(co...]
    unnamed x72 -> x59, local copies, waits for them, and re-layouts: 27.7 us -> 4.83 us
  transfers between devices with their start and end apart: 17 -> 26, of which waited for: 15 -> 4; matrix products, arithmetic and copies ran while one was open for 16% -> 2% of each run, Pallas kernels for 0% -> 64%
where the time goes in v1:
time: 296 us; the launch traced here: 295 us
  Pallas kernels  192 us (65%)
  waiting for transfers between devices  54.4 us (18%)
  starting transfers between devices  34.6 us (12%)
  local copies, waits for them, and re-layouts  10.4 us (4%)
  other arithmetic  3.17 us (1%)
    pallas_call x14, Pallas kernels, run_kernel(): pl.pallas_call(kernel, out_shape=[jax.ShapeDtypeStruct(shape, dtype) for...  192 us
    ppermute x23, waiting for transfers between devices, xor_swap(): lax.ppermute(value, axis, [(source, source ^ mask) for source in range(co...  51.7 us
    ppermute x23, starting transfers between devices, xor_swap(): lax.ppermute(value, axis, [(source, source ^ mask) for source in range(co...  26 us
    ppermute x1, starting transfers between devices, body(): arrived = lax.ppermute(travelling, 'col', pairs)  5.95 us
  transfers between devices with their start and end apart: 26, of which 4 were waited for; matrix products, arithmetic and copies ran while one was open for 2% of the time, Pallas kernels for 64%

profile of v1, /device:TPU:0, one launch (start us, length us, event | category | flops | bytes accessed | tf_op | source)
XLA Modules:
  0.0 295.4 jit_solution(2133851473499047654)
XLA Ops:
  1.5 5.9 %collective-permute-start = (f32[2,64,256]{2,1,0:T(8,128)S(1)}, f32[2,64,256]{2,1,0:T(8,128)S(1)}, u32[]{:S(2)}, u32[]{:S(2)}) collective-permute-start(f32[2,64,256]{2,1,0:T(8,128)S(1)} %slice_bitcast_fusion.5), channel_id=1, source_target_pairs={{0,4},{8,12},{16,20},{24,28}} | collective-permute-start | bytes 393224 | tf_op jit(solution)/shard_map/ppermute | solution.py:542
  7.5 1.4 copy.16
  9.5 4.6 %shard_map.51 = (f32[6,64,256]{2,1,0:T(8,128)}, f32[6,64,256]{2,1,0:T(8,128)}, f32[18,64,256]{2,1,0:T(8,128)}, f32[18,64,256]{2,1,0:T(8,128)}) custom-call(s32[8]{0:T(128)} %stack.38.refs_0_.scalar_ref, s32[10,5]{1,0:T(8,128)} %bitcast.36, f32[1,10,5,2,64,256]{5,4,3,2,1,0:T(8,128)} %refs_2_.3, f32[1,10,2,64,256]{4,3,2,1,0:T(8,128)} %refs_1_.1), custom_call_target="tpu_custom_call" | custom-call | bytes 3932276 | tf_op jit(solution)/shard_map/pallas_call | solution.py:46
  17.0 1.3 collective-permute-start.2
  18.3 1.3 collective-permute-start.1
  19.6 1.6 collective-permute-start.4
  21.2 2.7 collective-permute-done.2
  24.0 1.6 collective-permute-start.3
  25.6 1.5 collective-permute-start.9
  27.6 23.7 %collective-permute-done.3 = f32[6,64,256]{2,1,0:T(8,128)S(1)} collective-permute-done((f32[6,64,256]{2,1,0:T(8,128)S(1)}, f32[6,64,256]{2,1,0:T(8,128)S(1)}, u32[]{:S(2)}, u32[]{:S(2)}) %collective-permute-start.3) | collective-permute-done | bytes 393248 | tf_op jit(solution)/shard_map/ppermute | solution.py:22
  52.4 1.7 collective-permute-start.5
  54.1 8.8 %collective-permute-done.10 = f32[6,64,256]{2,1,0:T(8,128)S(1)} collective-permute-done((f32[6,64,256]{2,1,0:T(8,128)S(1)}, f32[6,64,256]{2,1,0:T(8,128)S(1)}, u32[]{:S(2)}, u32[]{:S(2)}) %collective-permute-start.10) | collective-permute-done | bytes 393248 | tf_op jit(solution)/shard_map/ppermute | solution.py:22
  64.0 19.1 %collective-permute-done.5.refs_4_ = f32[17,64,256]{2,1,0:T(8,128)S(1)} collective-permute-done((f32[17,64,256]{2,1,0:T(8,128)S(1)}, f32[17,64,256]{2,1,0:T(8,128)S(1)}, u32[]{:S(2)}, u32[]{:S(2)}) %collective-permute-start.5) | collective-permute-done | bytes 1114144 | tf_op jit(solution)/shard_map/ppermute | solution.py:22
  83.3 4.3 %shard_map.50 = (f32[10,64,128]{2,1,0:T(8,128)}, f32[10,64,128]{2,1,0:T(8,128)}, f32[10,64,128]{2,1,0:T(8,128)}, f32[10,64,128]{2,1,0:T(8,128)}, f32[10,64,128]{...) custom-call(s32[8]{0:T(128)} %stack.38.refs_0_.scalar_ref, ...), custom_call_target="tpu_custom_call" | custom-call | bytes 3276916 | tf_op jit(solution)/shard_map/pallas_call | solution.py:46
  87.6 1.6 collective-permute-start.16
  89.7 1.5 collective-permute-start.18
  91.2 1.5 collective-permute-start.6
  92.7 5.3 %shard_map.53 = (f32[768,512]{1,0:T(8,128)}, bf16[1536,256]{1,0:T(8,128)(2,1)}, bf16[1536,256]{1,0:T(8,128)(2,1)}, bf16[512,1024]{1,0:T(8,128)(2,1)}, bf16[512,1024]{1,0:T(8,128)(2,1)}) custom-call(s32[8]{0:T(128)} %stack.38.refs_0_.scalar_ref, f32[18,64,256]{2,1,0:T(8,128)} %get-tuple-element.85.refs_1_, f32[18,64,256]{2,1,0:T(8,128)} %copy-done.1, ...), custom_call_target="tpu_custom_call" | custom-call | bytes 2555920 | tf_op jit(solution)/shard_map/pallas_call | solution.py:46
  98.0 6.0 %shard_map.52 = (f32[1024,512]{1,0:T(8,128)}, bf16[2048,256]{1,0:T(8,128)(2,1)}, bf16[2048,256]{1,0:T(8,128)(2,1)}, bf16[512,1280]{1,0:T(8,128)(2,1)}, bf16[512,1280]{1,0:T(8,128)(2,1)}) custom-call(s32[8]{0:T(128)} %stack.38.refs_0_.scalar_ref, f32[18,64,256]{2,1,0:T(8,128)} %get-tuple-element.85.refs_1_, f32[18,64,256]{2,1,0:T(8,128)} %copy-done.1, ...), custom_call_target="tpu_custom_call" | custom-call | bytes 2326544 | tf_op jit(solution)/shard_map/pallas_call | solution.py:46
  105.1 5.1 %shard_map.54 = (bf16[512,256]{1,0:T(8,128)(2,1)}, bf16[512,256]{1,0:T(8,128)(2,1)}, f32[256,512]{1,0:T(8,128)}, bf16[512,256]{1,0:T(8,128)(2,1)}, bf16[512,256]...) custom-call(s32[8]{0:T(128)} %stack.38.refs_0_.scalar_ref, ...), custom_call_target="tpu_custom_call" | custom-call | bytes 1572880 | tf_op jit(solution)/shard_map/pallas_call | solution.py:46
  110.2 20.0 %shard_map.58 = (f32[4,2,64,256]{3,2,1,0:T(8,128)}, f32[2,64,256]{2,1,0:T(8,128)}, f32[4,2,64,256]{3,2,1,0:T(8,128)}, f32[2,64,256]{2,1,0:T(8,128)}) custom-call(s32[8]{0:T(128)} %stack.38.refs_0_.scalar_ref, f32[1024,512]{1,0:T(8,128)} %get-tuple-element.126.refs_1_, bf16[1536,256]{1,0:T(8,128)(2,1)} %get-tuple-element.88.refs_7_.refs_2_, ...), custom_call_target="tpu_custom_call" | custom-call | flops 8053063680 | bytes 12058640 | tf_op jit(solution)/shard_map/pallas_call | solution.py:46
  134.2 15.4 %shard_map.56 = (f32[5,2,64,128]{3,2,1,0:T(8,128)}, f32[5,2,64,128]{3,2,1,0:T(8,128)}, f32[5,2,64,128]{3,2,1,0:T(8,128)}, f32[5,2,64,128]{3,2,1,0:T(8,128)}, bf1...) custom-call(s32[8]{0:T(128)} %stack.38.refs_0_.scalar_ref, ...), custom_call_target="tpu_custom_call" | custom-call | flops 5033164800 | bytes 13762576 | tf_op jit(solution)/shard_map/pallas_call | solution.py:46
  149.6 1.6 collective-permute-start.19
  153.9 15.6 %shard_map.55 = (f32[5,2,64,128]{3,2,1,0:T(8,128)}, f32[5,2,64,128]{3,2,1,0:T(8,128)}, f32[5,2,64,128]{3,2,1,0:T(8,128)}, f32[5,2,64,128]{3,2,1,0:T(8,128)}, bf1...) custom-call(s32[8]{0:T(128)} %stack.38.refs_0_.scalar_ref, ...), custom_call_target="tpu_custom_call" | custom-call | flops 5033164800 | bytes 13762576 | tf_op jit(solution)/shard_map/pallas_call | solution.py:46
  169.5 1.6 collective-permute-start.13
  173.1 20.2 %shard_map.57 = (f32[3,2,64,256]{3,2,1,0:T(8,128)}, f32[2,64,256]{2,1,0:T(8,128)}, f32[2,2,64,256]{3,2,1,0:T(8,128)}, f32[2,64,256]{2,1,0:T(8,128)}, f32[1,2,64,256]{3,2,1,0:T(8,128)}, /*index=5*/f32[2,64,256]{2,1,0:T(8,128)}) custom-call(s32[8]{0:T(128)} %stack.38.refs_0_.scalar_ref, f32[768,512]{1,0:T(8,128)} %get-tuple-element.120.refs_1_, ...), custom_call_target="tpu_custom_call" | custom-call | flops 8053063680 | bytes 8388624 | tf_op jit(solution)/shard_map/pallas_call | solution.py:46
  193.3 5.5 %shard_map.62 = (f32[2,64,256]{2,1,0:T(8,128)}, f32[2,64,256]{2,1,0:T(8,128)}, f32[2,64,256]{2,1,0:T(8,128)}, f32[2,64,256]{2,1,0:T(8,128)}) custom-call(s32[8]{0:T(128)} %stack.38.refs_0_.scalar_ref, bf16[256,1280]{1,0:T(8,128)(2,1)} %get-tuple-element.134.refs_1_, bf16[256,1280]{1,0:T(8,128)(2,1)} %get-tuple-element.135.refs_2_, ...), custom_call_target="tpu_custom_call" | custom-call | flops 2013265920 | bytes 5242896 | tf_op jit(solution)/shard_map/pallas_call | solution.py:46
  199.6 3.5 %shard_map.59.refs_4_ = f32[1,10,5,2,64,256]{5,4,3,2,1,0:T(8,128)} custom-call(s32[8]{0:T(128)} %stack.38.refs_0_.scalar_ref, f32[1,2,64,256]{3,2,1,0:T(8,128)} %get-tuple-element.123.refs_1_, f32[2,2,64,256]{3,2,1,0:T(8,128)} %get-tuple-element.124.refs_2_, f32[3,2,64,256]{3,2,1,0:T(8,128)} %get-tuple-element.125.refs_3_, ...), custom_call_target="tpu_custom_call" | custom-call | bytes 917520 | tf_op jit(solution)/shard_map/pallas_call | solution.py:46
  203.2 1.6 collective-permute-start.23
  205.8 41.6 %shard_map.60.refs_4_ = f32[1,10,5,2,64,256]{5,4,3,2,1,0:T(8,128)} custom-call(s32[8]{0:T(128)} %stack.38.refs_0_.scalar_ref, f32[5,2,64,128]{3,2,1,0:T(8,128)} %get-tuple-element.116.refs_0_, f32[5,2,64,128]{3,2,1,0:T(8,128)} %copy-done.8, f32[5,2,64,128]{3,2,1,0:T(8,128)} %copy-done.9, ...), custom_call_target="tpu_custom_call", output_to_operand_aliasing={{}: (5, {})} | custom-call | bytes 3932176 | tf_op jit(solution)/shard_map/pallas_call | solution.py:46
  249.4 41.5 %shard_map.61 = f32[1,10,5,2,64,256]{5,4,3,2,1,0:T(8,128)} custom-call(s32[8]{0:T(128)} %stack.38.refs_0_.scalar_ref, f32[5,2,64,128]{3,2,1,0:T(8,128)} %get-tuple-element.104.refs_0_, f32[5,2,64,128]{3,2,1,0:T(8,128)} %copy-done.11, f32[5,2,64,128]{3,2,1,0:T(8,128)} %copy-done.12, f32[5,2,64,128]{3,2,1,0:T(8,128)} %copy-done.13, ...), custom_call_target="tpu_custom_call", output_to_operand_aliasing={{}: (5, {})} | custom-call | bytes 3932176 | tf_op jit(solution)/shard_map/pallas_call | solution.py:46
  292.4 3.0 %shard_map.63 = f32[1,10,2,64,256]{4,3,2,1,0:T(8,128)} custom-call(s32[8]{0:T(128)} %stack.38.refs_0_.scalar_ref, f32[1,10,2,64,256]{4,3,2,1,0:T(8,128)} %refs_1_.1, f32[2,64,256]{2,1,0:T(8,128)} %get-tuple-element.130.refs_2_, f32[2,64,256]{2,1,0:T(8,128)} %get-tuple-element.131.refs_3_, f32[2,64,256]{2,1,0:T(8,128)} %get-tuple-element.132.refs_4_, ...), custom_call_target="tpu_custom_call" | custom-call | bytes 1245200 | tf_op jit(solution)/shard_map/pallas_call | solution.py:46
  (113 shorter events, 22.8 us)
Async XLA Ops:
  1.5 13.6 %collective-permute-start = (f32[2,64,256]{2,1,0:T(8,128)S(1)}, f32[2,64,256]{2,1,0:T(8,128)S(1)}, u32[]{:S(2)}, u32[]{:S(2)}) collective-permute-start(f32[2,64,256]{2,1,0:T(8,128)S(1)} %slice_bitcast_fusion.5), channel_id=1, source_target_pairs={{0,4},{8,12},{16,20},{24,28}} | collective-permute-start | bytes 393224 | tf_op jit(solution)/shard_map/ppermute | solution.py:542
  14.1 9.7 %copy-start.7 = (f32[6,64,256]{2,1,0:T(8,128)S(1)}, f32[6,64,256]{2,1,0:T(8,128)}, u32[]{:S(2)}) copy-start(f32[6,64,256]{2,1,0:T(8,128)} %get-tuple-element.79) | copy-start | bytes 1179652
  15.2 10.4 %copy-start.3 = (f32[18,64,256]{2,1,0:T(8,128)S(1)}, f32[18,64,256]{2,1,0:T(8,128)}, u32[]{:S(2)}) copy-start(f32[18,64,256]{2,1,0:T(8,128)} %get-tuple-element.85.refs_1_) | copy-start | bytes 3538948
  17.0 6.9 %collective-permute-start.2 = (f32[6,64,256]{2,1,0:T(8,128)}, f32[6,64,256]{2,1,0:T(8,128)S(1)}, u32[]{:S(2)}, u32[]{:S(2)}) collective-permute-start(f32[6,64,256]{2,1,0:T(8,128)} %pad_maximum_fusion.3), channel_id=1, source_target_pairs={{0,3},{4,7},{8,11},{12,15},{16,19},{20,23},{24,27},{28,31}} | collective-permute-start | bytes 1179656 | tf_op jit(solution)/shard_map/ppermute | solution.py:551
  18.3 5.6 %collective-permute-start.1 = (f32[6,64,256]{2,1,0:T(8,128)}, f32[6,64,256]{2,1,0:T(8,128)S(1)}, u32[]{:S(2)}, u32[]{:S(2)}) collective-permute-start(f32[6,64,256]{2,1,0:T(8,128)} %pad_maximum_fusion.3), channel_id=1, source_target_pairs={{0,1},{4,5},{8,9},{12,13},{16,17},{20,21},{24,25},{28,29}} | collective-permute-start | bytes 1179656 | tf_op jit(solution)/shard_map/ppermute | solution.py:548
  19.6 31.7 %collective-permute-start.4 = (f32[18,64,256]{2,1,0:T(8,128)}, f32[18,64,256]{2,1,0:T(8,128)S(1)}, u32[]{:S(2)}, u32[]{:S(2)}) collective-permute-start(f32[18,64,256]{2,1,0:T(8,128)} %get-tuple-element.80), channel_id=1, source_target_pairs={{0,16},{8,24},{16,0},{24,8},{1,17},{9,25},{17,1},{25,9},{2,18},{10... | collective-permute-start | bytes 3538952 | tf_op jit(solution)/shard_map/ppermute | solution.py:22
  24.0 27.4 %collective-permute-start.3 = (f32[6,64,256]{2,1,0:T(8,128)S(1)}, f32[6,64,256]{2,1,0:T(8,128)S(1)}, u32[]{:S(2)}, u32[]{:S(2)}) collective-permute-start(f32[6,64,256]{2,1,0:T(8,128)S(1)} %get-tuple-element.147), channel_id=1, source_target_pairs={{0,16},{8,24},{16,0},{24,8},{1,17},{9,25},{17,1},{25,9},{2,18},{10... | collective-permute-start | bytes 1179656 | tf_op jit(solution)/shard_map/ppermute | solution.py:22
  25.6 37.4 %collective-permute-start.9 = (f32[18,64,256]{2,1,0:T(8,128)S(1)}, f32[18,64,256]{2,1,0:T(8,128)S(1)}, u32[]{:S(2)}, u32[]{:S(2)}) collective-permute-start(f32[18,64,256]{2,1,0:T(8,128)S(1)} %copy-done.3), channel_id=1, source_target_pairs={{0,8},{8,0},{16,24},{24,16},{1,9},{9,1},{17,25},{25,17},{2,10},{10... | collective-permute-start | bytes 3538952 | tf_op jit(solution)/shard_map/ppermute | solution.py:22
  27.1 35.8 %collective-permute-start.10 = (f32[6,64,256]{2,1,0:T(8,128)S(1)}, f32[6,64,256]{2,1,0:T(8,128)S(1)}, u32[]{:S(2)}, u32[]{:S(2)}) collective-permute-start(f32[6,64,256]{2,1,0:T(8,128)S(1)} %get-tuple-element.147), channel_id=1, source_target_pairs={{0,8},{8,0},{16,24},{24,16},{1,9},{9,1},{17,25},{25,17},{2,10},{10... | collective-permute-start | bytes 1179656 | tf_op jit(solution)/shard_map/ppermute | solution.py:22
  52.4 30.7 %collective-permute-start.5 = (f32[17,64,256]{2,1,0:T(8,128)S(1)}, f32[17,64,256]{2,1,0:T(8,128)S(1)}, u32[]{:S(2)}, u32[]{:S(2)}) collective-permute-start(f32[17,64,256]{2,1,0:T(8,128)S(1)} %pad_maximum_fusion), channel_id=1, source_target_pairs={{0,8},{8,0},{16,24},{24,16},{1,9},{9,1},{17,25},{25,17},{2,10},{10... | collective-permute-start | bytes 3342344 | tf_op jit(solution)/shard_map/ppermute | solution.py:22
  63.0 20.1 %collective-permute-start.11 = (f32[7,64,256]{2,1,0:T(8,128)S(1)}, f32[7,64,256]{2,1,0:T(8,128)S(1)}, u32[]{:S(2)}, u32[]{:S(2)}) collective-permute-start(f32[7,64,256]{2,1,0:T(8,128)S(1)} %pad_maximum_fusion.2), channel_id=1, source_target_pairs={{0,16},{8,24},{16,0},{24,8},{1,17},{9,25},{17,1},{25,9},{2,18},{10... | collective-permute-start | bytes 1376264 | tf_op jit(solution)/shard_map/ppermute | solution.py:22
  83.2 20.8 %collective-permute-start.12 = (f32[24,64,256]{2,1,0:T(8,128)S(1)}, f32[24,64,256]{2,1,0:T(8,128)S(1)}, u32[]{:S(2)}, u32[]{:S(2)}) collective-permute-start(f32[24,64,256]{2,1,0:T(8,128)S(1)} %slice_dynamic-update-slice_fusion.refs_1_), channel_id=1, source_target_pairs={{0,1},{1,0},{2,3},{3,2},{4,5},{5,4},{6,7},{7,6},{8,9},{9,8},{10,11... | collective-permute-start | bytes 4718600 | tf_op jit(solution)/shard_map/ppermute | solution.py:22
  87.6 43.8 %collective-permute-start.16 = (f32[10,64,128]{2,1,0:T(8,128)}, f32[10,64,128]{2,1,0:T(8,128)S(1)}, u32[]{:S(2)}, u32[]{:S(2)}) collective-permute-start(f32[10,64,128]{2,1,0:T(8,128)} %get-tuple-element.113), channel_id=1, source_target_pairs={{0,8},{8,0},{16,24},{24,16},{1,9},{9,1},{17,25},{25,17},{2,10},{10... | collective-permute-start | bytes 983048 | tf_op jit(solution)/shard_map/ppermute | solution.py:22
  89.2 43.2 %collective-permute-start.17 = (f32[10,64,128]{2,1,0:T(8,128)}, f32[10,64,128]{2,1,0:T(8,128)S(1)}, u32[]{:S(2)}, u32[]{:S(2)}) collective-permute-start(f32[10,64,128]{2,1,0:T(8,128)} %get-tuple-element.114), channel_id=1, source_target_pairs={{0,16},{8,24},{16,0},{24,8},{1,17},{9,25},{17,1},{25,9},{2,18},{10... | collective-permute-start | bytes 983048 | tf_op jit(solution)/shard_map/ppermute | solution.py:22
  89.7 43.8 %collective-permute-start.18 = (f32[10,64,128]{2,1,0:T(8,128)}, f32[10,64,128]{2,1,0:T(8,128)S(1)}, u32[]{:S(2)}, u32[]{:S(2)}) collective-permute-start(f32[10,64,128]{2,1,0:T(8,128)} %get-tuple-element.115), channel_id=1, source_target_pairs={{0,24},{8,16},{16,8},{24,0},{1,25},{9,17},{17,9},{25,1},{2,26},{10... | collective-permute-start | bytes 983048 | tf_op jit(solution)/shard_map/ppermute | solution.py:22
  91.2 60.0 %collective-permute-start.6 = (f32[10,64,128]{2,1,0:T(8,128)}, f32[10,64,128]{2,1,0:T(8,128)S(1)}, u32[]{:S(2)}, u32[]{:S(2)}) collective-permute-start(f32[10,64,128]{2,1,0:T(8,128)} %get-tuple-element.82), channel_id=1, source_target_pairs={{0,8},{8,0},{16,24},{24,16},{1,9},{9,1},{17,25},{25,17},{2,10},{10... | collective-permute-start | bytes 983048 | tf_op jit(solution)/shard_map/ppermute | solution.py:22
  98.0 6.0 %copy-start.19 = (f32[10,64,128]{2,1,0:T(8,128)S(1)}, f32[10,64,128]{2,1,0:T(8,128)}, u32[]{:S(2)}) copy-start(f32[10,64,128]{2,1,0:T(8,128)} %get-tuple-element.83) | copy-start | bytes 983044
  104.0 48.1 %collective-permute-start.7 = (f32[10,64,128]{2,1,0:T(8,128)S(1)}, f32[10,64,128]{2,1,0:T(8,128)S(1)}, u32[]{:S(2)}, u32[]{:S(2)}) collective-permute-start(f32[10,64,128]{2,1,0:T(8,128)S(1)} %copy-done.19), channel_id=1, source_target_pairs={{0,16},{8,24},{16,0},{24,8},{1,17},{9,25},{17,1},{25,9},{2,18},{10... | collective-permute-start | bytes 983048 | tf_op jit(solution)/shard_map/ppermute | solution.py:22
  110.2 21.2 %copy-start.17 = (f32[10,64,128]{2,1,0:T(8,128)S(1)}, f32[10,64,128]{2,1,0:T(8,128)}, u32[]{:S(2)}) copy-start(f32[10,64,128]{2,1,0:T(8,128)} %get-tuple-element.84) | copy-start | bytes 983044
  131.4 21.8 %collective-permute-start.8 = (f32[10,64,128]{2,1,0:T(8,128)S(1)}, f32[10,64,128]{2,1,0:T(8,128)S(1)}, u32[]{:S(2)}, u32[]{:S(2)}) collective-permute-start(f32[10,64,128]{2,1,0:T(8,128)S(1)} %copy-done.17), channel_id=1, source_target_pairs={{0,24},{8,16},{16,8},{24,0},{1,25},{9,17},{17,9},{25,1},{2,26},{10... | collective-permute-start | bytes 983048 | tf_op jit(solution)/shard_map/ppermute | solution.py:22
  132.4 39.6 %collective-permute-start.22 = (f32[5,2,64,256]{3,2,1,0:T(8,128)S(1)}, f32[5,2,64,256]{3,2,1,0:T(8,128)S(1)}, u32[]{:S(2)}, u32[]{:S(2)}) collective-permute-start(f32[5,2,64,256]{3,2,1,0:T(8,128)S(1)} %pad_maximum_fusion.1), channel_id=1, source_target_pairs={{0,16},{8,24},{16,0},{24,8},{1,17},{9,25},{17,1},{25,9},{2,18},{10... | collective-permute-start | bytes 1966088 | tf_op jit(solution)/shard_map/ppermute | solution.py:22
  149.6 21.5 %collective-permute-start.19 = (f32[5,2,64,128]{3,2,1,0:T(8,128)}, f32[5,2,64,128]{3,2,1,0:T(8,128)S(1)}, u32[]{:S(2)}, u32[]{:S(2)}) collective-permute-start(f32[5,2,64,128]{3,2,1,0:T(8,128)} %get-tuple-element.117), channel_id=1, source_target_pairs={{0,8},{8,0},{16,24},{24,16},{1,9},{9,1},{17,25},{25,17},{2,10},{10... | collective-permute-start | bytes 983048 | tf_op jit(solution)/shard_map/ppermute | solution.py:22
  151.2 52.0 %collective-permute-start.20 = (f32[5,2,64,128]{3,2,1,0:T(8,128)}, f32[5,2,64,128]{3,2,1,0:T(8,128)S(1)}, u32[]{:S(2)}, u32[]{:S(2)}) collective-permute-start(f32[5,2,64,128]{3,2,1,0:T(8,128)} %get-tuple-element.118), channel_id=1, source_target_pairs={{0,16},{8,24},{16,0},{24,8},{1,17},{9,25},{17,1},{25,9},{2,18},{10... | collective-permute-start | bytes 983048 | tf_op jit(solution)/shard_map/ppermute | solution.py:22
  152.1 52.6 %collective-permute-start.21 = (f32[5,2,64,128]{3,2,1,0:T(8,128)}, f32[5,2,64,128]{3,2,1,0:T(8,128)S(1)}, u32[]{:S(2)}, u32[]{:S(2)}) collective-permute-start(f32[5,2,64,128]{3,2,1,0:T(8,128)} %get-tuple-element.119), channel_id=1, source_target_pairs={{0,24},{8,16},{16,8},{24,0},{1,25},{9,17},{17,9},{25,1},{2,26},{10... | collective-permute-start | bytes 983048 | tf_op jit(solution)/shard_map/ppermute | solution.py:22
  169.5 77.9 %collective-permute-start.13 = (f32[5,2,64,128]{3,2,1,0:T(8,128)}, f32[5,2,64,128]{3,2,1,0:T(8,128)S(1)}, u32[]{:S(2)}, u32[]{:S(2)}) collective-permute-start(f32[5,2,64,128]{3,2,1,0:T(8,128)} %get-tuple-element.105), channel_id=1, source_target_pairs={{0,8},{8,0},{16,24},{24,16},{1,9},{9,1},{17,25},{25,17},{2,10},{10... | collective-permute-start | bytes 983048 | tf_op jit(solution)/shard_map/ppermute | solution.py:22
  171.1 22.2 %copy-start.8 = (f32[5,2,64,128]{3,2,1,0:T(8,128)}, f32[5,2,64,128]{3,2,1,0:T(8,128)S(1)}, u32[]{:S(2)}) copy-start(f32[5,2,64,128]{3,2,1,0:T(8,128)S(1)} %collective-permute-done.19.refs_1_) | copy-start | bytes 983044
  171.1 77.5 %collective-permute-start.14 = (f32[5,2,64,128]{3,2,1,0:T(8,128)}, f32[5,2,64,128]{3,2,1,0:T(8,128)S(1)}, u32[]{:S(2)}, u32[]{:S(2)}) collective-permute-start(f32[5,2,64,128]{3,2,1,0:T(8,128)} %get-tuple-element.106), channel_id=1, source_target_pairs={{0,16},{8,24},{16,0},{24,8},{1,17},{9,25},{17,1},{25,9},{2,18},{10... | collective-permute-start | bytes 983048 | tf_op jit(solution)/shard_map/ppermute | solution.py:22
  172.0 76.5 %collective-permute-start.15 = (f32[5,2,64,128]{3,2,1,0:T(8,128)}, f32[5,2,64,128]{3,2,1,0:T(8,128)S(1)}, u32[]{:S(2)}, u32[]{:S(2)}) collective-permute-start(f32[5,2,64,128]{3,2,1,0:T(8,128)} %get-tuple-element.107), channel_id=1, source_target_pairs={{0,24},{8,16},{16,8},{24,0},{1,25},{9,17},{17,9},{25,1},{2,26},{10... | collective-permute-start | bytes 983048 | tf_op jit(solution)/shard_map/ppermute | solution.py:22
  203.2 88.4 %collective-permute-start.23 = (f32[2,64,256]{2,1,0:T(8,128)S(1)}, f32[2,64,256]{2,1,0:T(8,128)S(1)}, u32[]{:S(2)}, u32[]{:S(2)}) collective-permute-start(f32[2,64,256]{2,1,0:T(8,128)S(1)} %copy-done.27), channel_id=1, source_target_pairs={{0,8},{8,0},{16,24},{24,16},{1,9},{9,1},{17,25},{25,17},{2,10},{10... | collective-permute-start | bytes 393224 | tf_op jit(solution)/shard_map/ppermute | solution.py:22
  204.7 86.9 %collective-permute-start.24 = (f32[2,64,256]{2,1,0:T(8,128)S(1)}, f32[2,64,256]{2,1,0:T(8,128)S(1)}, u32[]{:S(2)}, u32[]{:S(2)}) collective-permute-start(f32[2,64,256]{2,1,0:T(8,128)S(1)} %copy-done.26), channel_id=1, source_target_pairs={{0,16},{8,24},{16,0},{24,8},{1,17},{9,25},{17,1},{25,9},{2,18},{10... | collective-permute-start | bytes 393224 | tf_op jit(solution)/shard_map/ppermute | solution.py:22
  205.8 41.7 %copy-start.25 = (f32[2,64,256]{2,1,0:T(8,128)S(1)}, f32[2,64,256]{2,1,0:T(8,128)}, u32[]{:S(2)}) copy-start(f32[2,64,256]{2,1,0:T(8,128)} %get-tuple-element.145) | copy-start | bytes 393220
  247.5 44.2 %collective-permute-start.25 = (f32[2,64,256]{2,1,0:T(8,128)S(1)}, f32[2,64,256]{2,1,0:T(8,128)S(1)}, u32[]{:S(2)}, u32[]{:S(2)}) collective-permute-start(f32[2,64,256]{2,1,0:T(8,128)S(1)} %copy-done.25), channel_id=1, source_target_pairs={{0,24},{8,16},{16,8},{24,0},{1,25},{9,17},{17,9},{25,1},{2,26},{10... | collective-permute-start | bytes 393224 | tf_op jit(solution)/shard_map/ppermute | solution.py:22
  (22 other events, 41.6 us)
